TPU v7x, 32 devices: a whole 2x2x4 slice. The times are simulated.
32 devices in a mesh: parts: 2 (over y), track: 4 (over z), tm: 2 (over x), coef: 2 (over core).
Axes of the slice: x: 2, y: 2, z: 4, core: 2. Of those that a mesh axis runs over, the one named last changes fastest.
Arguments:
- sector_ids: int32 [12288], P(('parts', 'track', 'tm')), parts along dimension 0, may hold values from 0 to 63, as said below
- observed: float32 [3, 12288], P(None, ('parts', 'track', 'tm')), parts along dimension 1, may hold values from -6 to 6
- weights: float32 [3, 12288], P(None, ('parts', 'track', 'tm')), parts along dimension 1, may hold values from 0.3 to 3
- coefficients: float32 [2048, 128], P(('parts', 'track')), parts along dimension 0, may hold values from -6 to 6
- tile_index: int32 [128, 12], P(('parts', 'track', 'tm'), 'coef'), parts along dimension 0, may hold values from 0 to 1023, as said below
- tile_count: int32 [128], P(('parts', 'track', 'tm')), parts along dimension 0, may hold values from 3 to 12
- sensitivity: bfloat16 [128, 12, 3, 128, 128], P(('parts', 'track', 'tm'), 'coef'), parts along dimension 0, may hold values from -0.15625 to 0.15625
Outputs:
- gradient: float32 [2048, 128], P(('parts', 'track')), parts along dimension 0
There are 2 independent parts, one for each index of `parts`. A program takes and returns all parts, laid end to end along the dimension named above; each array names one. Nothing has to cross between parts.
Inputs may be any that keep to these rules, and one draw needn't show every extreme that they name: `sector_ids`: the rows of one index of track and tm fall in at most 192 rows into the 8 consecutive sectors of any one index, and some pair reaches 192; the sectors of each index receive exactly 768 rows in all; each sector holds at most 128 rows, and every index holds a sector with exactly 128. `tile_index`: entries at positions from tile_count on are arbitrary blocks and take no part. Block n belongs to track index n // 256. Of the 48 entries held by one index of track, tm and coef (its sectors' rows, its coef share of the columns), live or not, at most 24 name blocks of any one track index, and every such device has a track index named exactly 24 times.
All inputs are finite; a program needn't handle non-finite values.
Results may differ from a plain program's by a relative error of at most 0.0037.
Values may be sent and summed in bfloat16 or wider, within the bound.
A program may use at most 64 MiB of HBM per device.

v0:
```python
import jax
import jax.numpy as jnp
from jax import lax
from jax.sharding import PartitionSpec as P

HUBER = 2.0


def per_device(sector_ids, observed, weights, coefficients, tile_index, tile_count, sensitivity):
    sector_total = tile_index.shape[0]
    half_k = tile_index.shape[1]
    slot_count = sensitivity.shape[3]
    block_width = sensitivity.shape[4]
    owners = lax.axis_size(("track", "tm"))
    row_total = sector_ids.shape[0]
    capacity = 2 * row_total // owners
    rounded = coefficients.astype(jnp.bfloat16)
    every_block = lax.all_gather(rounded, "track", axis=0, tiled=True)
    owner_of = sector_ids // sector_total
    local_sector = sector_ids % sector_total
    onehot = (owner_of[:, None] == jnp.arange(owners, dtype=jnp.int32)[None, :]).astype(jnp.int32)
    ranking = jnp.sum((jnp.cumsum(onehot, axis=0) - 1) * onehot, axis=1)
    placing = owner_of * capacity + ranking
    payload = jnp.concatenate([observed, weights], axis=0)
    outgoing = jnp.zeros((6, owners * capacity), jnp.float32).at[:, placing].set(payload)
    outgoing = jnp.transpose(outgoing.reshape(6, owners, capacity), (1, 0, 2))
    labels = jnp.full((owners * capacity,), -1, jnp.int32).at[placing].set(local_sector)
    labels = labels.reshape(owners, capacity)
    got_rows, got_labels = (
        lax.all_to_all(outgoing, ("track", "tm"), split_axis=0, concat_axis=0, tiled=True),
        lax.all_to_all(labels, ("track", "tm"), split_axis=0, concat_axis=0, tiled=True),
    )
    received = jnp.transpose(got_rows, (1, 0, 2)).reshape(6, owners * capacity)
    flat_labels = got_labels.reshape(owners * capacity)
    member = (flat_labels[:, None] == jnp.arange(sector_total, dtype=jnp.int32)[None, :]).astype(
        jnp.int32
    )
    within = jnp.sum((jnp.cumsum(member, axis=0) - 1) * member, axis=1)
    target = jnp.where(
        flat_labels >= 0, flat_labels * slot_count + within, sector_total * slot_count
    )
    gridded = jnp.zeros((6, sector_total * slot_count + 1), jnp.float32).at[:, target].set(received)
    gridded = jnp.transpose(gridded[:, :-1].reshape(6, sector_total, slot_count), (1, 0, 2))
    observed_tiles = gridded[:, :3]
    weight_tiles = gridded[:, 3:]
    k_global = lax.axis_index("coef") * half_k + jnp.arange(half_k, dtype=jnp.int32)
    active = k_global[None, :] < tile_count[:, None]
    blocks = jnp.take(every_block, tile_index, axis=0)
    blocks = jnp.where(active[:, :, None], blocks, jnp.zeros_like(blocks))
    partial_pred = jnp.einsum(
        "skcjb,skb->scj", sensitivity, blocks, preferred_element_type=jnp.float32
    )
    predicted = lax.psum(partial_pred, "coef")
    scaled = weight_tiles * (predicted - observed_tiles)
    force = (weight_tiles * scaled / jnp.sqrt(1.0 + (scaled / HUBER) ** 2)).astype(jnp.bfloat16)
    tile_grad = jnp.einsum("skcjb,scj->skb", sensitivity, force, preferred_element_type=jnp.float32)
    tile_grad = jnp.where(active[:, :, None], tile_grad, jnp.zeros_like(tile_grad))
    block_total = every_block.shape[0]
    partial_grad = jnp.zeros((block_total, block_width), jnp.float32)
    partial_grad = partial_grad.at[tile_index.reshape(-1)].add(tile_grad.reshape(-1, block_width))
    summed = lax.psum_scatter(partial_grad, "track", scatter_dimension=0, tiled=True)
    gradient = lax.psum(summed, ("tm", "coef"))
    return gradient


def solution(mesh):
    placed = (
        P(("parts", "track", "tm")),
        P(None, ("parts", "track", "tm")),
        P(None, ("parts", "track", "tm")),
        P(("parts", "track"), None),
        P(("parts", "track", "tm"), "coef"),
        P(("parts", "track", "tm")),
        P(("parts", "track", "tm"), "coef", None, None, None),
    )
    return jax.shard_map(
        per_device,
        mesh=mesh,
        in_specs=placed,
        out_specs=P(("parts", "track"), None),
        check_vma=False,
    )
```

profile of v0, /device:TPU:0, one launch (start us, length us, event | category | flops | bytes accessed | tf_op | source)
XLA Modules:
  0.0 135.0 jit_solution(9949122944024813271)
XLA Ops:
  6.5 0.7 add_select_fusion
  7.2 1.7 %reduce-window.14 = s32[8,6,128]{2,0,1:T(8,128)S(1)} reduce-window(s32[8,6,128]{2,0,1:T(8,128)S(1)} %fusion.13, s32[]{:T(128)} %constant.40.clone.1), window={size=1x1x128 pad=0_0x0_0x127_0}, to_apply=%region_0.1 | reduce-window | flops 780288 | bytes 49156 | tf_op jit(solution)/shard_map/reduce-window
  8.9 0.1 slice.30
  9.0 0.1 copy.24
  9.2 0.2 reduce-window.15
  9.3 0.1 copy.25
  9.4 0.1 fusion.11
  9.5 3.4 %scatter_custom_fusion = s32[1536]{0:T(1024)S(1)} fusion(s32[768]{0:T(1024)S(1)} %compare_select_fusion.2, s32[768]{0:T(1024)S(1)} %get-tuple-element.7, s32[]{:T(128)} %constant.74.clone.1), kind=kCustom, calls=%fused_computation.50 | custom fusion | bytes 6148 | tf_op jit(solution)/shard_map/scatter | solution.py:27
  12.9 0.7 all_to_all.9
  13.6 7.3 %all-to-all-start = ((s32[8,1,192]{2,1,0:T(1,128)}), s32[8,1,192]{2,1,0:T(1,128)S(1)}, u32[]{:S(2)}, u32[]{:S(2)}) async-start(s32[8,1,192]{2,1,0:T(1,128)} %all_to_all.9), calls=%async_computation | async-start | bytes 16384 | tf_op jit(solution)/shard_map/all_to_all | solution.py:31
  20.8 0.7 compare_select_fusion.1
  21.5 0.8 reshape.166
  22.3 0.7 maximum_bitcast_fusion
  23.0 0.2 copy.26
  23.2 4.4 %scatter_custom_fusion.1 = f32[6,1536]{0,1:T(8,128)S(1)} fusion(s32[768]{0:T(1024)S(1)} %compare_select_fusion.2, f32[768,6]{1,0:T(8,128)S(1)} %copy.26, f32[]{:T(128)} %constant.39.clone.1), kind=kCustom, calls=%fused_computation.7 | custom fusion | bytes 36868 | tf_op jit(solution)/shard_map/scatter | solution.py:25
  27.6 1.0 copy.27
  28.6 0.9 convert_element_type.18
  29.5 14.5 %all_gather.3 = bf16[1024,128]{1,0:T(8,128)(2,1)S(1)} all-gather(bf16[256,128]{1,0:T(8,128)(2,1)S(1)} %convert_element_type.18), channel_id=1, replica_groups=mesh['parts'=2,'track'=4,'tm'=2,'coef'=2] {'track'}, dimensions={0}, use_global_device_ids=true | all-gather | bytes 327680 | tf_op jit(solution)/shard_map/all_gather | solution.py:18
  44.0 0.1 reshape.175
  44.0 0.6 gather_fusion
  44.7 0.8 compare_and_fusion
  45.4 0.1 select_bitcast_fusion
  45.5 3.7 %fusion = f32[8,1,3,128,1]{3,1,4,2,0:T(1,128)S(1)} fusion(bf16[8,6,3,128,128]{4,3,2,1,0:T(8,128)(2,1)} %param.13, bf16[8,6,128,1,1]{2,1,0,3,4:T(8,128)(2,1)S(1)} %select_bitcast_fusion), kind=kOutput, calls=%fused_computation.5 | convolution fusion | flops 4718592 | bytes 4743168 | tf_op jit(solution)/shard_map/skcjb,skb->scj/dot_general | solution.py:50
  49.2 3.3 %psum.14 = f32[8,3,128]{2,0,1:T(8,128)S(1)} all-reduce(f32[8,3,128]{2,0,1:T(8,128)S(1)} %bitcast.50), channel_id=1, replica_groups=mesh['parts'=2,'track'=4,'tm'=2,'coef'=2] {'coef'}, use_global_device_ids=true, to_apply=%region_9.10 | all-reduce | flops 3072 | bytes 24576 | tf_op jit(solution)/shard_map/psum | solution.py:53
  52.5 0.0 all-to-all-done
  52.5 5.7 %all-to-all-start.1 = ((f32[8,6,192]{2,1,0:T(8,128)}), f32[8,6,192]{2,1,0:T(8,128)S(1)}, u32[]{:S(2)}, u32[]{:S(2)}) async-start(f32[8,6,192]{2,1,0:T(8,128)} %bitcast.8), calls=%async_computation.1 | async-start | bytes 131072 | tf_op jit(solution)/shard_map/all_to_all | solution.py:30
  58.2 0.0 reduce-scatter.2.cloned.1.call-start
  58.3 0.1 eq.61
  58.4 0.1 eq.57
  58.5 2.3 %reduce-window.16 = s32[8,12,128]{2,1,0:T(8,128)S(1)} reduce-window(s32[8,12,128]{2,1,0:T(8,128)S(1)} %fusion.8, s32[]{:T(128)} %constant.40.clone.1), window={size=1x1x128 pad=0_0x0_0x127_0}, to_apply=%region_4.5 | reduce-window | flops 1560576 | bytes 98308 | tf_op jit(solution)/shard_map/reduce-window.2
  60.7 0.3 slice_reduce_fusion
  61.0 0.2 reduce-window.19
  61.2 0.1 add_bitcast_fusion
  61.3 0.1 mul.43
  61.4 0.1 ge.21
  61.6 3.5 %all-to-all-done.1 = f32[8,6,192]{2,1,0:T(8,128)S(1)} async-done(((f32[8,6,192]{2,1,0:T(8,128)}), f32[8,6,192]{2,1,0:T(8,128)S(1)}, u32[]{:S(2)}, u32[]{:S(2)}) %all-to-all-start.1) | async-done | bytes 36896 | tf_op jit(solution)/shard_map/all_to_all | solution.py:30
  65.1 0.1 reshape.198
  65.2 0.3 copy.29
  65.5 4.4 %scatter_custom_fusion.2 = f32[6,1025]{0,1:T(8,128)S(1)} fusion(s32[1536]{0:T(1024)S(1)} %fusion.17, f32[1536,6]{1,0:T(8,128)S(1)} %copy.29, f32[]{:T(128)} %constant.39.clone.1), kind=kCustom, calls=%fused_computation.9 | custom fusion | bytes 24604 | tf_op jit(solution)/shard_map/scatter | solution.py:42
  70.0 0.2 copy.36
  70.2 3.1 %fusion.15 = f32[8,1,6,128,1]{3,1,4,2,0:T(1,128)S(1)} fusion(bf16[8,6,3,128,128]{4,3,2,1,0:T(8,128)(2,1)} %param.13, bf16[8,3,128,1,1]{2,0,1,3,4:T(8,128)(2,1)S(1)} %fusion.18), kind=kOutput, calls=%fused_computation.34 | convolution fusion | flops 4718592 | bytes 4749312 | tf_op jit(solution)/shard_map/skcjb,scj->skb/dot_general | solution.py:56
  73.3 0.1 bitcast_select_fusion
  73.4 1.5 %scatter_custom_fusion.3 = f32[1024,128]{1,0:T(8,128)} fusion(s32[48]{0:T(128)S(1)} %fusion.23, f32[48,128]{1,0:T(8,128)S(1)} %reshape.209, f32[]{:T(128)} %constant.39.clone.1), kind=kCustom, calls=%fused_computation.11 | custom fusion | flops 6144 | bytes 524292 | tf_op jit(solution)/shard_map/scatter-add | solution.py:60
  74.9 0.0 reduce-scatter.2.cloned.1.call-update
  75.0 0.0 all-reduce.2.cloned.1.call-start
  75.0 19.6 %reduce-scatter.2.cloned.1.call-done = f32[256,128]{1,0:T(8,128)} async-done(((f32[1024,128]{1,0:T(8,128)}), f32[256,128]{1,0:T(8,128)}) %reduce-scatter.2.cloned.1.call-update) | async-done | bytes 131088 | tf_op jit(solution)/shard_map/reduce_scatter | solution.py:61
  94.6 0.0 all-reduce.2.cloned.1.call-update
  94.7 32.0 %all-reduce.2.cloned.1.call-done = f32[256,128]{1,0:T(8,128)} async-done(((f32[256,128]{1,0:T(8,128)}), f32[256,128]{1,0:T(8,128)}) %all-reduce.2.cloned.1.call-update) | async-done | bytes 131088 | tf_op jit(solution)/shard_map/psum | solution.py:62
  126.6 1.6 %copy.49 = f32[256,128]{1,0:T(8,128)} copy(f32[256,128]{1,0:T(8,128)} %all-reduce.2.cloned.1.call-done) | data formatting | bytes 262144
  (16 shorter events, 0.3 us)
Async XLA Ops:
  13.6 38.9 %all-to-all-start = ((s32[8,1,192]{2,1,0:T(1,128)}), s32[8,1,192]{2,1,0:T(1,128)S(1)}, u32[]{:S(2)}, u32[]{:S(2)}) async-start(s32[8,1,192]{2,1,0:T(1,128)} %all_to_all.9), calls=%async_computation | async-start | bytes 16384 | tf_op jit(solution)/shard_map/all_to_all | solution.py:31
  52.5 12.6 %all-to-all-start.1 = ((f32[8,6,192]{2,1,0:T(8,128)}), f32[8,6,192]{2,1,0:T(8,128)S(1)}, u32[]{:S(2)}, u32[]{:S(2)}) async-start(f32[8,6,192]{2,1,0:T(8,128)} %bitcast.8), calls=%async_computation.1 | async-start | bytes 131072 | tf_op jit(solution)/shard_map/all_to_all | solution.py:30
  58.2 36.4 %reduce-scatter.2.cloned.1.call-start = ((), (), s32[]{:S(2)}) async-start(), calls=%async_computation.3 | async-start | bytes 655360 | tf_op jit(solution)/shard_map/reduce_scatter | solution.py:61
  75.0 51.7 %all-reduce.2.cloned.1.call-start = ((), (), s32[]{:S(2)}) async-start(), calls=%async_computation.4 | async-start | bytes 262144 | tf_op jit(solution)/shard_map/psum | solution.py:62
Sparse Core Ops, SparseCore 0:
  75.1 19.5 reduce-scatter.1
  97.0 29.6 all-reduce.1
where the time goes:
time: 136 us; the launch traced here: 135 us
  waiting for transfers between devices  55.2 us (41%)
  local copies, waits for them, and re-layouts  18.6 us (14%)
  blocking collectives  17.8 us (13%)
  between operations  13.5 us (10%)
  starting transfers between devices  13.1 us (10%)
  other arithmetic  10.2 us (7%)
  matrix products  6.73 us (5%)
    psum x1, waiting for transfers between devices, per_device(): gradient = lax.psum(summed, ('tm', 'coef'))  32 us
    reduce_scatter x1, waiting for transfers between devices, per_device(): lax.psum_scatter(partial_grad, 'track', scatter_dimension=0, tiled=True)  19.6 us
    all_gather x1, blocking collectives, per_device(): every_block = lax.all_gather(rounded, 'track', axis=0, tiled=True)  14.5 us
    all_to_all x1, starting transfers between devices, per_device(): lax.all_to_all(labels, ('track', 'tm'), split_axis=0, concat_axis=0, tile...  7.25 us
    all_to_all x1, starting transfers between devices, per_device(): lax.all_to_all(outgoing, ('track', 'tm'), split_axis=0, concat_axis=0, ti...  5.72 us
    scatter x1, local copies, waits for them, and re-layouts, per_device(): jnp.zeros((6, sector_total * slot_count + 1), jnp.float32).at[:, target]  4.45 us
    scatter x1, local copies, waits for them, and re-layouts, per_device(): jnp.zeros((6, owners * capacity), jnp.float32).at[:, placing].set(payload)  4.36 us
    another operation x4, other arithmetic  4.31 us
  transfers between devices with their start and end apart: 4, of which 3 were waited for; matrix products, arithmetic and copies ran while one was open for 13% of the time, Pallas kernels for 0%

commit v1 on v0

--- a/solution.py
+++ b/solution.py
@@ -59,7 +59,8 @@
     partial_grad = jnp.zeros((block_total, block_width), jnp.float32)
     partial_grad = partial_grad.at[tile_index.reshape(-1)].add(tile_grad.reshape(-1, block_width))
     summed = lax.psum_scatter(partial_grad, "track", scatter_dimension=0, tiled=True)
-    gradient = lax.psum(summed, ("tm", "coef"))
+    shards = lax.all_gather(summed, ("tm", "coef"))
+    gradient = jnp.sum(shards, axis=0)
     return gradient
 
 

time: 136 us -> 110 us (0.81)
  waiting for transfers between devices: 55.2 us -> 23.2 us
  blocking collectives: 17.8 us -> 25.1 us
  local copies, waits for them, and re-layouts: 18.6 us -> 17 us
    psum x1 -> x0, waiting for transfers between devices: 32 us -> none  [per_device(): gradient = lax.psum(summed, ('tm', 'coef'))]
    all_gather x0 -> x1, blocking collectives: none -> 7.33 us  [per_device(): shards = lax.all_gather(summed, ('tm', 'coef'))]
    unnamed x1 -> x0, local copies, waits for them, and re-layouts: 1.57 us -> none
  transfers between devices with their start and end apart: 4 -> 3, of which waited for: 3 -> 2; matrix products, arithmetic and copies ran while one was open for 13% -> 16% of each run, Pallas kernels for 0% -> 0%
where the time goes in v1:
time: 110 us; the launch traced here: 109 us
  blocking collectives  25.1 us (23%)
  waiting for transfers between devices  23.2 us (21%)
  local copies, waits for them, and re-layouts  17 us (15%)
  between operations  13.5 us (12%)
  starting transfers between devices  13 us (12%)
  other arithmetic  10.9 us (10%)
  matrix products  6.73 us (6%)
    reduce_scatter x1, waiting for transfers between devices, per_device(): lax.psum_scatter(partial_grad, 'track', scatter_dimension=0, tiled=True)  19.7 us
    all_gather x1, blocking collectives, per_device(): every_block = lax.all_gather(rounded, 'track', axis=0, tiled=True)  14.5 us
    all_gather x1, blocking collectives, per_device(): shards = lax.all_gather(summed, ('tm', 'coef'))  7.33 us
    all_to_all x1, starting transfers between devices, per_device(): lax.all_to_all(labels, ('track', 'tm'), split_axis=0, concat_axis=0, tile...  7.25 us
    all_to_all x1, starting transfers between devices, per_device(): lax.all_to_all(outgoing, ('track', 'tm'), split_axis=0, concat_axis=0, ti...  5.72 us
    scatter x1, local copies, waits for them, and re-layouts, per_device(): jnp.zeros((6, sector_total * slot_count + 1), jnp.float32).at[:, target]  4.45 us
    scatter x1, local copies, waits for them, and re-layouts, per_device(): jnp.zeros((6, owners * capacity), jnp.float32).at[:, placing].set(payload)  4.36 us
    another operation x4, other arithmetic  4.31 us
  transfers between devices with their start and end apart: 3, of which 2 were waited for; matrix products, arithmetic and copies ran while one was open for 16% of the time, Pallas kernels for 0%

profile of v1, /device:TPU:0, one launch (start us, length us, event | category | flops | bytes accessed | tf_op | source)
XLA Modules:
  0.0 109.5 jit_solution(10149785270307628693)
XLA Ops:
  6.5 0.7 add_select_fusion
  7.2 1.7 %reduce-window.14 = s32[8,6,128]{2,0,1:T(8,128)S(1)} reduce-window(s32[8,6,128]{2,0,1:T(8,128)S(1)} %fusion.13, s32[]{:T(128)} %constant.40.clone.1), window={size=1x1x128 pad=0_0x0_0x127_0}, to_apply=%region_0.1 | reduce-window | flops 780288 | bytes 49156 | tf_op jit(solution)/shard_map/reduce-window
  8.9 0.1 slice.30
  9.0 0.1 copy.30
  9.2 0.2 reduce-window.15
  9.3 0.1 copy.31
  9.4 0.1 fusion.11
  9.5 3.4 %scatter_custom_fusion = s32[1536]{0:T(1024)S(1)} fusion(s32[768]{0:T(1024)S(1)} %compare_select_fusion.2, s32[768]{0:T(1024)S(1)} %get-tuple-element.7, s32[]{:T(128)} %constant.44.clone.1), kind=kCustom, calls=%fused_computation.50 | custom fusion | bytes 6148 | tf_op jit(solution)/shard_map/scatter | solution.py:27
  12.9 0.7 all_to_all.9
  13.6 7.3 %all-to-all-start = ((s32[8,1,192]{2,1,0:T(1,128)}), s32[8,1,192]{2,1,0:T(1,128)S(1)}, u32[]{:S(2)}, u32[]{:S(2)}) async-start(s32[8,1,192]{2,1,0:T(1,128)} %all_to_all.9), calls=%async_computation | async-start | bytes 16384 | tf_op jit(solution)/shard_map/all_to_all | solution.py:31
  20.8 0.7 compare_select_fusion.1
  21.5 0.8 reshape.166
  22.3 0.7 maximum_bitcast_fusion
  23.0 0.2 copy.32
  23.2 4.4 %scatter_custom_fusion.1 = f32[6,1536]{0,1:T(8,128)S(1)} fusion(s32[768]{0:T(1024)S(1)} %compare_select_fusion.2, f32[768,6]{1,0:T(8,128)S(1)} %copy.32, f32[]{:T(128)} %constant.39.clone.1), kind=kCustom, calls=%fused_computation.7 | custom fusion | bytes 36868 | tf_op jit(solution)/shard_map/scatter | solution.py:25
  27.6 1.0 copy.33
  28.6 0.9 convert_element_type.18
  29.5 14.5 %all_gather.9 = bf16[1024,128]{1,0:T(8,128)(2,1)S(1)} all-gather(bf16[256,128]{1,0:T(8,128)(2,1)S(1)} %convert_element_type.18), channel_id=1, replica_groups=mesh['parts'=2,'track'=4,'tm'=2,'coef'=2] {'track'}, dimensions={0}, use_global_device_ids=true | all-gather | bytes 327680 | tf_op jit(solution)/shard_map/all_gather | solution.py:18
  44.0 0.1 reshape.175
  44.0 0.6 gather_fusion
  44.7 0.8 compare_and_fusion
  45.4 0.1 select_bitcast_fusion
  45.5 3.7 %fusion = f32[8,1,3,128,1]{3,1,4,2,0:T(1,128)S(1)} fusion(bf16[8,6,3,128,128]{4,3,2,1,0:T(8,128)(2,1)} %param.13, bf16[8,6,128,1,1]{2,1,0,3,4:T(8,128)(2,1)S(1)} %select_bitcast_fusion), kind=kOutput, calls=%fused_computation.5 | convolution fusion | flops 4718592 | bytes 4743168 | tf_op jit(solution)/shard_map/skcjb,skb->scj/dot_general | solution.py:50
  49.2 3.3 %psum.7 = f32[8,3,128]{2,0,1:T(8,128)S(1)} all-reduce(f32[8,3,128]{2,0,1:T(8,128)S(1)} %bitcast.52), channel_id=1, replica_groups=mesh['parts'=2,'track'=4,'tm'=2,'coef'=2] {'coef'}, use_global_device_ids=true, to_apply=%region_9.10 | all-reduce | flops 3072 | bytes 24576 | tf_op jit(solution)/shard_map/psum | solution.py:53
  52.5 0.0 all-to-all-done
  52.5 5.7 %all-to-all-start.1 = ((f32[8,6,192]{2,1,0:T(8,128)}), f32[8,6,192]{2,1,0:T(8,128)S(1)}, u32[]{:S(2)}, u32[]{:S(2)}) async-start(f32[8,6,192]{2,1,0:T(8,128)} %bitcast.8), calls=%async_computation.1 | async-start | bytes 131072 | tf_op jit(solution)/shard_map/all_to_all | solution.py:30
  58.2 0.0 reduce-scatter.2.cloned.1.call-start
  58.3 0.1 eq.61
  58.4 0.1 eq.57
  58.5 2.3 %reduce-window.16 = s32[8,12,128]{2,1,0:T(8,128)S(1)} reduce-window(s32[8,12,128]{2,1,0:T(8,128)S(1)} %fusion.8, s32[]{:T(128)} %constant.40.clone.1), window={size=1x1x128 pad=0_0x0_0x127_0}, to_apply=%region_4.5 | reduce-window | flops 1560576 | bytes 98308 | tf_op jit(solution)/shard_map/reduce-window.2
  60.7 0.3 slice_reduce_fusion
  61.0 0.2 reduce-window.19
  61.2 0.1 add_bitcast_fusion
  61.3 0.1 mul.43
  61.4 0.1 ge.21
  61.6 3.5 %all-to-all-done.1 = f32[8,6,192]{2,1,0:T(8,128)S(1)} async-done(((f32[8,6,192]{2,1,0:T(8,128)}), f32[8,6,192]{2,1,0:T(8,128)S(1)}, u32[]{:S(2)}, u32[]{:S(2)}) %all-to-all-start.1) | async-done | bytes 36896 | tf_op jit(solution)/shard_map/all_to_all | solution.py:30
  65.1 0.1 reshape.198
  65.2 0.3 copy.35
  65.5 4.4 %scatter_custom_fusion.2 = f32[6,1025]{0,1:T(8,128)S(1)} fusion(s32[1536]{0:T(1024)S(1)} %fusion.17, f32[1536,6]{1,0:T(8,128)S(1)} %copy.35, f32[]{:T(128)} %constant.39.clone.1), kind=kCustom, calls=%fused_computation.9 | custom fusion | bytes 24604 | tf_op jit(solution)/shard_map/scatter | solution.py:42
  70.0 0.2 copy.42
  70.2 3.1 %fusion.15 = f32[8,1,6,128,1]{3,1,4,2,0:T(1,128)S(1)} fusion(bf16[8,6,3,128,128]{4,3,2,1,0:T(8,128)(2,1)} %param.13, bf16[8,3,128,1,1]{2,0,1,3,4:T(8,128)(2,1)S(1)} %fusion.18), kind=kOutput, calls=%fused_computation.34 | convolution fusion | flops 4718592 | bytes 4749312 | tf_op jit(solution)/shard_map/skcjb,scj->skb/dot_general | solution.py:56
  73.3 0.1 bitcast_select_fusion
  73.4 1.5 %scatter_custom_fusion.3 = f32[1024,128]{1,0:T(8,128)} fusion(s32[48]{0:T(128)S(1)} %fusion.23, f32[48,128]{1,0:T(8,128)S(1)} %reshape.209, f32[]{:T(128)} %constant.39.clone.1), kind=kCustom, calls=%fused_computation.11 | custom fusion | flops 6144 | bytes 524292 | tf_op jit(solution)/shard_map/scatter-add | solution.py:60
  74.9 0.0 reduce-scatter.2.cloned.1.call-update
  75.0 19.7 %reduce-scatter.2.cloned.1.call-done = f32[256,128]{1,0:T(8,128)} async-done(((f32[1024,128]{1,0:T(8,128)}), f32[256,128]{1,0:T(8,128)}) %reduce-scatter.2.cloned.1.call-update) | async-done | bytes 131088 | tf_op jit(solution)/shard_map/reduce_scatter | solution.py:61
  94.6 7.3 %all-gather = f32[1024,128]{1,0:T(8,128)S(1)} all-gather(f32[256,128]{1,0:T(8,128)} %reduce-scatter.2.cloned.1.call-done), channel_id=2, replica_groups=mesh['parts'=2,'track'=4,'tm'=2,'coef'=2] {'tm','coef'}, dimensions={0}, use_global_device_ids=true | all-gather | bytes 655360 | tf_op jit(solution)/shard_map/all_gather | solution.py:62
  102.0 0.7 reduce_sum.32
  (16 shorter events, 0.3 us)
Async XLA Ops:
  13.6 38.9 %all-to-all-start = ((s32[8,1,192]{2,1,0:T(1,128)}), s32[8,1,192]{2,1,0:T(1,128)S(1)}, u32[]{:S(2)}, u32[]{:S(2)}) async-start(s32[8,1,192]{2,1,0:T(1,128)} %all_to_all.9), calls=%async_computation | async-start | bytes 16384 | tf_op jit(solution)/shard_map/all_to_all | solution.py:31
  52.5 12.6 %all-to-all-start.1 = ((f32[8,6,192]{2,1,0:T(8,128)}), f32[8,6,192]{2,1,0:T(8,128)S(1)}, u32[]{:S(2)}, u32[]{:S(2)}) async-start(f32[8,6,192]{2,1,0:T(8,128)} %bitcast.8), calls=%async_computation.1 | async-start | bytes 131072 | tf_op jit(solution)/shard_map/all_to_all | solution.py:30
  58.2 36.4 %reduce-scatter.2.cloned.1.call-start = ((), (), s32[]{:S(2)}) async-start(), calls=%async_computation.3 | async-start | bytes 655360 | tf_op jit(solution)/shard_map/reduce_scatter | solution.py:61
Sparse Core Ops, SparseCore 0:
  75.1 19.5 reduce-scatter.1
